TPU v7x, 256 devices: a whole 4x4x8 slice. The times are simulated.
256 devices in a mesh: gx: 4 (over y), gy: 4 (over x), gz: 16 (over z, core).
Axes of the slice: x: 4, y: 4, z: 8, core: 2. Of those that a mesh axis runs over, the one named last changes fastest.
Arguments:
- activations: bfloat16 [4, 4, 4, 16, 16, 64, 128], P('gx', 'gy', None, None, None, 'gz'), may hold values from -6 to 6
- cotangent: bfloat16 [4, 4, 4, 16, 16, 64, 128], P('gx', 'gy', None, None, None, 'gz'), may hold values from -6 to 6
- tap_weights: bfloat16 [9, 128, 128], replicated, may hold values from -0.1875 to 0.1875
- depth_tap_weight: bfloat16 [5, 128], replicated, may hold values from -2.5 to 2.5
- counts: int32 [4, 4], P('gx', 'gy'), may hold values from 2 to 4, as said below
- neighbors: int32 [4, 4, 4, 8], P('gx', 'gy'), may hold values from 0 to 36, as said below
Outputs:
- output: bfloat16 [4, 4, 4, 16, 16, 64, 128], P('gx', 'gy', None, None, None, 'gz')
- input_grad: bfloat16 [4, 4, 4, 16, 16, 64, 128], P('gx', 'gy', None, None, None, 'gz')
- tap_grad: float32 [9, 128, 128], replicated
- depth_grad: float32 [5, 128], replicated
Inputs may be any that keep to these rules, and one draw needn't show every extreme that they name: Slots 0 to counts - 1 of an owner are occupied; one owner has all 4 slots occupied. `neighbors`: each owner holds a grid of 3 x 3 block column positions; the owners tile the plane along gx and gy. Directions d = 0..7 are (-1,-1), (-1,0), (-1,1), (0,-1), (0,1), (1,-1), (1,0), (1,1) in (x, y). For an occupied slot the entry names the occupied column at the adjacent position as ((ox' + 1) * 3 + oy' + 1) * 4 + slot, with (ox', oy') the offset of its owner; 36 marks an empty or outside position and every direction of an unoccupied slot. The relation is geometric, hence symmetric.
All inputs are finite; a program needn't handle non-finite values.
Results may differ from a plain program's by a relative error of at most 0.005.
Values may be sent and summed in bfloat16 or wider, within the bound.
A program may use at most 128 MiB of HBM per device.

v0:
```python
import jax
import jax.numpy as jnp
from jax import lax
from jax.sharding import PartitionSpec as P


def padded_2(cells, sides, width):
    for axis, dim in sides:
        count = lax.axis_size(axis)
        ends = count - 1
        head = lax.slice_in_dim(cells, 0, width, axis=dim)
        tail = lax.slice_in_dim(cells, cells.shape[dim] - width, cells.shape[dim], axis=dim)
        cells = jnp.concatenate(
            [
                lax.ppermute(tail, axis, [(i, (i + 1) % count) for i in range(ends)]),
                cells,
                lax.ppermute(head, axis, [((i + 1) % count, i) for i in range(ends)]),
            ],
            axis=dim,
        )
    return cells


def rims_of(tile):
    last_idx = tile.shape[-4] - 1
    edge_rows = jnp.concatenate(
        [
            tile[..., 0, :, :, :],
            tile[..., last_idx, :, :, :],
            tile[..., :, 0, :, :],
            tile[..., :, last_idx, :, :],
        ],
        axis=-3,
    )
    corner_cells = jnp.stack(
        [
            tile[..., 0, 0, :, :],
            tile[..., 0, last_idx, :, :],
            tile[..., last_idx, 0, :, :],
            tile[..., last_idx, last_idx, :, :],
        ],
        axis=-3,
    )
    return jnp.concatenate([edge_rows, corner_cells], axis=-3)


def assemble(center, pooled, neighbor_ids):
    tile_len = center.shape[1]
    chosen = [pooled[neighbor_ids[:, direction]] for direction in range(8)]

    def edge_of(direction, which):
        return chosen[direction][:, which * tile_len : (which + 1) * tile_len]

    def corner_of(direction, which):
        return chosen[direction][:, 4 * tile_len + which : 4 * tile_len + which + 1]

    top_row = jnp.concatenate([corner_of(0, 3), edge_of(1, 1), corner_of(2, 2)], axis=1)
    bottom_row = jnp.concatenate([corner_of(5, 1), edge_of(6, 0), corner_of(7, 0)], axis=1)
    middle = jnp.concatenate([edge_of(3, 3)[:, :, None], center, edge_of(4, 2)[:, :, None]], axis=2)
    return jnp.concatenate([top_row[:, None], middle, bottom_row[:, None]], axis=1)


def neighbor_pool(tile):
    capacity = tile.shape[2]
    extended = rims_of(padded_2(tile, (("gx", 0), ("gy", 1)), 1))
    pooled = extended.reshape((9 * capacity,) + extended.shape[3:])
    return jnp.concatenate([pooled, jnp.zeros((1,) + pooled.shape[1:], pooled.dtype)], axis=0)


def convolve(padded, tap_weights):
    tile_len = padded.shape[1] - 2
    channels = padded.shape[-1]
    shape_out = padded.shape[:1] + (tile_len, tile_len) + padded.shape[3:]
    summed = jnp.zeros(shape_out, jnp.float32)
    for row_tap in range(3):
        for col_tap in range(3):
            window = padded[:, row_tap : row_tap + tile_len, col_tap : col_tap + tile_len]
            summed = summed + jnp.dot(
                window.reshape(-1, channels),
                tap_weights[3 * row_tap + col_tap],
                preferred_element_type=jnp.float32,
            ).reshape(shape_out)
    return summed


def convolve_back(padded, tap_weights):
    tile_len = padded.shape[1] - 2
    channels = padded.shape[-1]
    shape_out = padded.shape[:1] + (tile_len, tile_len) + padded.shape[3:]
    summed = jnp.zeros(shape_out, jnp.float32)
    for row_tap in range(3):
        for col_tap in range(3):
            window = padded[
                :, 2 - row_tap : 2 - row_tap + tile_len, 2 - col_tap : 2 - col_tap + tile_len
            ]
            summed = summed + jnp.dot(
                window.reshape(-1, channels),
                tap_weights[3 * row_tap + col_tap].T,
                preferred_element_type=jnp.float32,
            ).reshape(shape_out)
    return summed


def tap_gradient(padded, grad_center):
    tile_len = padded.shape[1] - 2
    channels = padded.shape[-1]
    grad_rows = grad_center.reshape(-1, channels)
    parts = []
    for row_tap in range(3):
        for col_tap in range(3):
            window = padded[:, row_tap : row_tap + tile_len, col_tap : col_tap + tile_len]
            parts.append(
                lax.dot_general(
                    window.reshape(-1, channels),
                    grad_rows,
                    (((0,), (0,)), ((), ())),
                    preferred_element_type=jnp.float32,
                )
            )
    return jnp.stack(parts, axis=0)


def z_padded(field, dilation):
    widths = [(0, 0)] * field.ndim
    widths[-2] = (2 * dilation, 2 * dilation)
    return jnp.pad(field, widths)


def depth_forward_pass(field, depth_tap_weight, dilation):
    length = field.shape[-2]
    padded = z_padded(field, dilation)
    summed = jnp.zeros(field.shape, jnp.float32)
    for tap_idx in range(5):
        window = lax.slice_in_dim(
            padded, tap_idx * dilation, tap_idx * dilation + length, axis=field.ndim - 2
        )
        summed = summed + depth_tap_weight[tap_idx].astype(jnp.float32) * window.astype(jnp.float32)
    return summed


def depth_backward_pass(field, depth_tap_weight, dilation):
    length = field.shape[-2]
    padded = z_padded(field, dilation)
    summed = jnp.zeros(field.shape, jnp.float32)
    for tap_idx in range(5):
        start = (4 - tap_idx) * dilation
        window = lax.slice_in_dim(padded, start, start + length, axis=field.ndim - 2)
        summed = summed + depth_tap_weight[tap_idx].astype(jnp.float32) * window.astype(jnp.float32)
    return summed


def depth_weight_gradient(active_columns, grads, dilation):
    length = active_columns.shape[-2]
    padded = z_padded(active_columns, dilation)
    grads_float = grads.astype(jnp.float32)
    axes_all = tuple(range(active_columns.ndim - 1))
    parts = []
    for tap_idx in range(5):
        window = lax.slice_in_dim(
            padded, tap_idx * dilation, tap_idx * dilation + length, axis=active_columns.ndim - 2
        )
        parts.append(jnp.sum(window.astype(jnp.float32) * grads_float, axis=axes_all))
    return jnp.stack(parts, axis=0)


def gather_columns(field):
    return lax.all_to_all(field, "gz", split_axis=1, concat_axis=2, tiled=True)


def spread_slabs(field):
    return lax.all_to_all(field, "gz", split_axis=2, concat_axis=1, tiled=True)


def body(activations, cotangent, tap_weights, depth_tap_weight, counts, neighbors):
    capacity = activations.shape[2]
    tile_len = activations.shape[3]
    slab_len = activations.shape[5]
    channels = activations.shape[6]
    live_mask = jnp.arange(capacity, dtype=jnp.int32) < counts[0, 0]
    live_float = live_mask.astype(jnp.float32)[:, None, None, None, None]
    masked = jnp.where(
        live_mask[None, None, :, None, None, None, None],
        activations,
        jnp.zeros((), activations.dtype),
    )
    table = neighbors[0, 0]
    center = masked[0, 0]
    padded_x = assemble(center, neighbor_pool(masked), table)
    pre_act = convolve(padded_x, tap_weights)
    active_columns = (jax.nn.silu(pre_act) * live_float).astype(jnp.bfloat16)
    flat_active = active_columns.reshape(capacity, tile_len * tile_len, slab_len, channels)
    flat_grad = cotangent.reshape(capacity, tile_len * tile_len, slab_len, channels)
    dilation = slab_len * lax.axis_size("gz") // 4
    column_active = gather_columns(flat_active)
    slab_out = spread_slabs(
        depth_forward_pass(column_active, depth_tap_weight, dilation).astype(jnp.bfloat16)
    )
    column_grad = gather_columns(flat_grad)
    depth_partial = depth_weight_gradient(column_active, column_grad, dilation)
    slab_back = spread_slabs(
        depth_backward_pass(column_grad, depth_tap_weight, dilation).astype(jnp.bfloat16)
    )
    tile_shape = (capacity, tile_len, tile_len, slab_len, channels)
    output = (center.astype(jnp.float32) + slab_out.reshape(tile_shape).astype(jnp.float32)).astype(
        jnp.bfloat16
    )
    sigma = jax.nn.sigmoid(pre_act)
    grad_pre = (
        slab_back.reshape(tile_shape).astype(jnp.float32)
        * sigma
        * (1.0 + pre_act * (1.0 - sigma))
        * live_float
    ).astype(jnp.bfloat16)
    padded_g = assemble(grad_pre, neighbor_pool(grad_pre[None, None]), table)
    back_conv = convolve_back(padded_g, tap_weights)
    input_grad = ((cotangent[0, 0].astype(jnp.float32) + back_conv) * live_float).astype(
        jnp.bfloat16
    )
    tap_part = tap_gradient(padded_x, grad_pre)
    tap_grad, depth_grad = lax.psum((tap_part, depth_partial), ("gx", "gy", "gz"))
    return (output[None, None], input_grad[None, None], tap_grad, depth_grad)


def solution(mesh):
    placed = (
        P("gx", "gy", None, None, None, "gz", None),
        P("gx", "gy", None, None, None, "gz", None),
        P(),
        P(),
        P("gx", "gy"),
        P("gx", "gy", None, None),
    )
    return jax.shard_map(
        body,
        mesh=mesh,
        in_specs=placed,
        out_specs=(
            P("gx", "gy", None, None, None, "gz", None),
            P("gx", "gy", None, None, None, "gz", None),
            P(),
            P(),
        ),
        check_vma=False,
    )
```

profile of v0, /device:TPU:1, one launch (start us, length us, event | category | flops | bytes accessed | tf_op | source)
XLA Modules:
  0.0 494.8 jit_solution(9856210542787049037)
XLA Ops:
  10.6 4.7 collective-permute-start
  16.7 9.9 %all-to-all-start.2 = ((bf16[4,256,4,128]{3,2,0,1:T(4,128)(2,1)}), bf16[4,256,4,128]{3,2,0,1:T(4,128)(2,1)}, u32[]{:S(2)}, u32[]{:S(2)}) async-start(bf16[4,256,4,128]{3,2,0,1:T(4,128)(2,1)} %bitcast.285), calls=%async_computation.2 | async-start | bytes 2097152 | tf_op jit(solution)/shard_map/all_to_all | solution.py:167
  26.6 7.5 %collective-permute-done.1 = bf16[1,1,4,16,16,4,128]{6,4,5,3,2,1,0:T(8,128)(2,1)S(1)} collective-permute-done((bf16[1,1,4,16,16,4,128]{6,4,5,3,2,1,0:T(8,128)(2,1)S(1)}, bf16[1,1,4,16,16,4,128]{6,4,5,3,2,1,0:T(8,128)(2,1)S(1)}, u32[]{:S(2)}, u32[]{:S(2)}) %collective-permute-start.1) | collective-permute-done | bytes 1048608 | tf_op jit(solution)/shard_map/ppermute | solution.py:17
  38.1 7.5 %collective-permute-start.2 = (bf16[3,1,4,16,16,4,128]{6,4,5,3,2,1,0:T(8,128)(2,1)}, bf16[3,1,4,16,16,4,128]{6,4,5,3,2,1,0:T(8,128)(2,1)}, u32[]{:S(2)}, u32[]{:S(2)}) collective-permute-start(bf16[3,1,4,16,16,4,128]{6,4,5,3,2,1,0:T(8,128)(2,1)} %pad_maximum_fusion), channel_id=1, source_target_pairs={{0,16},{16,32},{32,48},{1,17},{17,33},{33,49},{2,18},{18,34},{34,5... | collective-permute-start | bytes 9437192 | tf_op jit(solution)/shard_map/ppermute | solution.py:15
  45.7 8.9 %all-to-all-done.2 = bf16[4,256,4,128]{3,2,0,1:T(4,128)(2,1)} async-done(((bf16[4,256,4,128]{3,2,0,1:T(4,128)(2,1)}), bf16[4,256,4,128]{3,2,0,1:T(4,128)(2,1)}, u32[]{:S(2)}, u32[]{:S(2)}) %all-to-all-start.2) | async-done | bytes 1048608 | tf_op jit(solution)/shard_map/all_to_all | solution.py:167
  60.5 4.9 all-to-all-start.3
  69.9 22.8 %all-to-all-done.3 = bf16[4,16,64,128]{3,1,0,2:T(8,128)(2,1)} async-done(((bf16[4,16,64,128]{3,1,0,2:T(8,128)(2,1)}), bf16[4,16,64,128]{3,1,0,2:T(8,128)(2,1)}, u32[]{:S(2)}, u32[]{:S(2)}) %all-to-all-start.3) | async-done | bytes 1048608 | tf_op jit(solution)/shard_map/all_to_all | solution.py:171
  92.7 2.9 copy.167
  95.6 12.9 %collective-permute-done.3 = bf16[3,1,4,16,16,4,128]{6,4,5,3,2,1,0:T(8,128)(2,1)} collective-permute-done((bf16[3,1,4,16,16,4,128]{6,4,5,3,2,1,0:T(8,128)(2,1)}, bf16[3,1,4,16,16,4,128]{6,4,5,3,2,1,0:T(8,128)(2,1)}, u32[]{:S(2)}, u32[]{:S(2)}) %collective-permute-start.3) | collective-permute-done | bytes 3145760 | tf_op jit(solution)/shard_map/ppermute | solution.py:17
  111.9 5.0 %pad_maximum_fusion.6 = (bf16[3,3,4,16,1,4,128]{6,4,5,3,2,1,0:T(2,128)(2,1)S(1)}, bf16[3,3,4,16,1,4,128]{6,4,5,3,2,1,0:T(2,128)(2,1)S(1)}) fusion(bf16[3,1,4,16,16,4,128]{6,4,5,3,2,1,0:T(8,128)(2,1)} %collective-permute-done.3, bf16[3,1,4,16,16,4,128]{6,4,5,3,2,1,0:T(8,128)(2,1)} %collective-permute-done.2, ...), kind=kLoop, calls=%fused_computation.64 | loop fusion | flops 5898240 | bytes 10616832 | tf_op jit(solution)/shard_map/slice | solution.py:31
  130.2 2.6 gather_fusion.4
  132.9 2.6 gather_fusion.3
  135.7 2.6 gather_fusion.2
  154.8 11.9 %all-to-all-start = ((bf16[4,256,4,128]{3,2,0,1:T(4,128)(2,1)}), bf16[4,256,4,128]{3,2,0,1:T(4,128)(2,1)}, u32[]{:S(2)}, u32[]{:S(2)}) async-start(bf16[4,256,4,128]{3,2,0,1:T(4,128)(2,1)} %copy.157), calls=%async_computation | async-start | bytes 2097152 | tf_op jit(solution)/shard_map/all_to_all | solution.py:167
  169.6 4.9 collective-permute-start.4
  176.0 19.8 %collective-permute-done.5 = bf16[1,1,4,16,16,4,128]{6,4,5,3,2,1,0:T(8,128)(2,1)S(1)} collective-permute-done((bf16[1,1,4,16,16,4,128]{6,4,5,3,2,1,0:T(8,128)(2,1)S(1)}, bf16[1,1,4,16,16,4,128]{6,4,5,3,2,1,0:T(8,128)(2,1)S(1)}, u32[]{:S(2)}, u32[]{:S(2)}) %collective-permute-start.5) | collective-permute-done | bytes 1048608 | tf_op jit(solution)/shard_map/ppermute | solution.py:17
  200.1 6.5 %collective-permute-start.6 = (bf16[3,1,4,16,16,4,128]{6,4,5,3,2,1,0:T(8,128)(2,1)}, bf16[3,1,4,16,16,4,128]{6,4,5,3,2,1,0:T(8,128)(2,1)}, u32[]{:S(2)}, u32[]{:S(2)}) collective-permute-start(bf16[3,1,4,16,16,4,128]{6,4,5,3,2,1,0:T(8,128)(2,1)} %pad_maximum_fusion.1), channel_id=1, source_target_pairs={{0,16},{16,32},{32,48},{1,17},{17,33},{33,49},{2,18},{18,34},{34,5... | collective-permute-start | bytes 9437192 | tf_op jit(solution)/shard_map/ppermute | solution.py:15
  215.0 8.1 %all-to-all-start.1 = ((bf16[4,16,64,128]{3,1,0,2:T(8,128)(2,1)}), bf16[4,16,64,128]{3,1,0,2:T(8,128)(2,1)}, u32[]{:S(2)}, u32[]{:S(2)}) async-start(bf16[4,16,64,128]{3,1,0,2:T(8,128)(2,1)} %copy.160), calls=%async_computation.1 | async-start | bytes 2097152 | tf_op jit(solution)/shard_map/all_to_all | solution.py:171
  223.2 2.7 fusion.20
  233.3 111.5 %psum.15 = f32[5,128]{1,0:T(8,128)} all-reduce(f32[5,128]{1,0:T(8,128)S(1)} %stack.63), channel_id=1, replica_groups=mesh['gx'=4,'gy'=4,'gz'=16] {'gx','gy','gz'}, use_global_device_ids=true, to_apply=%region_6.7 | all-reduce | flops 640 | bytes 5120 | tf_op jit(solution)/shard_map/psum | solution.py:220
  350.8 5.1 %pad_maximum_fusion.4 = (bf16[3,3,4,16,1,4,128]{6,4,5,3,2,1,0:T(2,128)(2,1)S(1)}, bf16[3,3,4,16,1,4,128]{6,4,5,3,2,1,0:T(2,128)(2,1)S(1)}) fusion(bf16[3,1,4,16,16,4,128]{6,4,5,3,2,1,0:T(8,128)(2,1)} %collective-permute-done.7, bf16[3,1,4,16,16,4,128]{6,4,5,3,2,1,0:T(8,128)(2,1)} %collective-permute-done.6, ...), kind=kLoop, calls=%fused_computation.62 | loop fusion | flops 5898240 | bytes 10616832 | tf_op jit(solution)/shard_map/slice | solution.py:31
  361.4 3.2 gather_fusion.15
  367.2 3.2 gather_fusion.13
  393.6 92.2 %all-reduce.6.cloned.1.call-done = f32[9,128,128]{2,1,0:T(8,128)} async-done(((f32[9,128,128]{2,1,0:T(8,128)}), f32[9,128,128]{2,1,0:T(8,128)}) %all-reduce.6.cloned.1.call-update) | async-done | bytes 589840 | tf_op jit(solution)/shard_map/psum | solution.py:220
  (216 shorter events, 114.6 us)
Async XLA Ops:
  7.2 8.2 %copy-start.17 = (bf16[1,1,4,16,16,4,128]{6,5,4,3,2,1,0:T(4,128)(2,1)S(1)}, bf16[1,1,4,16,16,4,128]{6,5,4,3,2,1,0:T(4,128)(2,1)}, u32[]{:S(2)}) copy-start(bf16[1,1,4,16,16,4,128]{6,5,4,3,2,1,0:T(4,128)(2,1)} %param.7) | copy-start | bytes 3145732
  9.3 24.8 %collective-permute-start.1 = (bf16[1,1,4,16,16,4,128]{6,4,5,3,2,1,0:T(8,128)(2,1)S(1)}, bf16[1,1,4,16,16,4,128]{6,4,5,3,2,1,0:T(8,128)(2,1)S(1)}, u32[]{:S(2)}, u32[]{:S(2)}) collective-permute-start(bf16[1,1,4,16,16,4,128]{6,4,5,3,2,1,0:T(8,128)(2,1)S(1)} %copy_select_fusion), channel_id=1, source_target_pairs={{64,0},{128,64},{192,128},{65,1},{129,65},{193,129},{66,2},{130,66... | collective-permute-start | bytes 3145736 | tf_op jit(solution)/shard_map/ppermute | solution.py:17
  10.6 24.2 %collective-permute-start = (bf16[1,1,4,16,16,4,128]{6,4,5,3,2,1,0:T(8,128)(2,1)S(1)}, bf16[1,1,4,16,16,4,128]{6,4,5,3,2,1,0:T(8,128)(2,1)S(1)}, u32[]{:S(2)}, u32[]{:S(2)}) collective-permute-start(bf16[1,1,4,16,16,4,128]{6,4,5,3,2,1,0:T(8,128)(2,1)S(1)} %copy_select_fusion), channel_id=1, source_target_pairs={{0,64},{64,128},{128,192},{1,65},{65,129},{129,193},{2,66},{66,130... | collective-permute-start | bytes 3145736 | tf_op jit(solution)/shard_map/ppermute | solution.py:15
  16.7 37.9 %all-to-all-start.2 = ((bf16[4,256,4,128]{3,2,0,1:T(4,128)(2,1)}), bf16[4,256,4,128]{3,2,0,1:T(4,128)(2,1)}, u32[]{:S(2)}, u32[]{:S(2)}) async-start(bf16[4,256,4,128]{3,2,0,1:T(4,128)(2,1)} %bitcast.285), calls=%async_computation.2 | async-start | bytes 2097152 | tf_op jit(solution)/shard_map/all_to_all | solution.py:167
  26.6 19.1 %copy-start.26 = (bf16[5,128]{1,0:T(8,128)(2,1)S(1)}, bf16[5,128]{1,0:T(8,128)(2,1)}, u32[]{:S(2)}) copy-start(bf16[5,128]{1,0:T(8,128)(2,1)} %param.9) | copy-start | bytes 3844
  36.9 71.7 %collective-permute-start.3 = (bf16[3,1,4,16,16,4,128]{6,4,5,3,2,1,0:T(8,128)(2,1)}, bf16[3,1,4,16,16,4,128]{6,4,5,3,2,1,0:T(8,128)(2,1)}, u32[]{:S(2)}, u32[]{:S(2)}) collective-permute-start(bf16[3,1,4,16,16,4,128]{6,4,5,3,2,1,0:T(8,128)(2,1)} %pad_maximum_fusion), channel_id=1, source_target_pairs={{16,0},{32,16},{48,32},{17,1},{33,17},{49,33},{18,2},{34,18},{50,3... | collective-permute-start | bytes 9437192 | tf_op jit(solution)/shard_map/ppermute | solution.py:17
  38.1 71.3 %collective-permute-start.2 = (bf16[3,1,4,16,16,4,128]{6,4,5,3,2,1,0:T(8,128)(2,1)}, bf16[3,1,4,16,16,4,128]{6,4,5,3,2,1,0:T(8,128)(2,1)}, u32[]{:S(2)}, u32[]{:S(2)}) collective-permute-start(bf16[3,1,4,16,16,4,128]{6,4,5,3,2,1,0:T(8,128)(2,1)} %pad_maximum_fusion), channel_id=1, source_target_pairs={{0,16},{16,32},{32,48},{1,17},{17,33},{33,49},{2,18},{18,34},{34,5... | collective-permute-start | bytes 9437192 | tf_op jit(solution)/shard_map/ppermute | solution.py:15
  60.5 7.6 %copy-start.19 = (bf16[9,128,128]{2,1,0:T(8,128)(2,1)S(1)}, bf16[9,128,128]{2,1,0:T(8,128)(2,1)}, u32[]{:S(2)}) copy-start(bf16[9,128,128]{2,1,0:T(8,128)(2,1)} %param.8) | copy-start | bytes 884740
  60.5 32.2 %all-to-all-start.3 = ((bf16[4,16,64,128]{3,1,0,2:T(8,128)(2,1)}), bf16[4,16,64,128]{3,1,0,2:T(8,128)(2,1)}, u32[]{:S(2)}, u32[]{:S(2)}) async-start(bf16[4,16,64,128]{3,1,0,2:T(8,128)(2,1)} %copy.166), calls=%async_computation.3 | async-start | bytes 2097152 | tf_op jit(solution)/shard_map/all_to_all | solution.py:171
  130.1 13.3 %copy-start = (bf16[4,16,16,4,128]{4,2,3,1,0:T(8,128)(2,1)S(1)}, bf16[4,16,16,4,128]{4,2,3,1,0:T(8,128)(2,1)}, u32[]{:S(2)}) copy-start(bf16[4,16,16,4,128]{4,2,3,1,0:T(8,128)(2,1)} %fusion.124) | copy-start | bytes 3145732
  132.9 11.6 %copy-start.20 = (bf16[4,16,1,4,128]{4,2,3,1,0:T(2,128)(2,1)}, bf16[4,16,1,4,128]{4,2,3,1,0:T(2,128)(2,1)S(1)}, u32[]{:S(2)}) copy-start(bf16[4,16,1,4,128]{4,2,3,1,0:T(2,128)(2,1)S(1)} %copy.150) | copy-start | bytes 196612
  135.7 8.9 %copy-start.22 = (bf16[4,16,1,4,128]{4,2,3,1,0:T(2,128)(2,1)}, bf16[4,16,1,4,128]{4,2,3,1,0:T(2,128)(2,1)S(1)}, u32[]{:S(2)}) copy-start(bf16[4,16,1,4,128]{4,2,3,1,0:T(2,128)(2,1)S(1)} %copy.149) | copy-start | bytes 196612
  154.8 54.6 %all-to-all-start = ((bf16[4,256,4,128]{3,2,0,1:T(4,128)(2,1)}), bf16[4,256,4,128]{3,2,0,1:T(4,128)(2,1)}, u32[]{:S(2)}, u32[]{:S(2)}) async-start(bf16[4,256,4,128]{3,2,0,1:T(4,128)(2,1)} %copy.157), calls=%async_computation | async-start | bytes 2097152 | tf_op jit(solution)/shard_map/all_to_all | solution.py:167
  166.7 7.8 %copy-start.6 = (bf16[4,17,18,4,128]{4,2,3,1,0:T(8,128)(2,1)S(1)}, bf16[4,17,18,4,128]{4,2,3,1,0:T(8,128)(2,1)}, u32[]{:S(2)}) copy-start(bf16[4,17,18,4,128]{4,2,3,1,0:T(8,128)(2,1)} %copy-done.5) | copy-start | bytes 3760132
  168.3 27.6 %collective-permute-start.5 = (bf16[1,1,4,16,16,4,128]{6,4,5,3,2,1,0:T(8,128)(2,1)S(1)}, bf16[1,1,4,16,16,4,128]{6,4,5,3,2,1,0:T(8,128)(2,1)S(1)}, u32[]{:S(2)}, u32[]{:S(2)}) collective-permute-start(bf16[1,1,4,16,16,4,128]{6,4,5,3,2,1,0:T(8,128)(2,1)S(1)} %bitcast.268), channel_id=1, source_target_pairs={{64,0},{128,64},{192,128},{65,1},{129,65},{193,129},{66,2},{130,66... | collective-permute-start | bytes 3145736 | tf_op jit(solution)/shard_map/ppermute | solution.py:17
  169.6 27.2 %collective-permute-start.4 = (bf16[1,1,4,16,16,4,128]{6,4,5,3,2,1,0:T(8,128)(2,1)S(1)}, bf16[1,1,4,16,16,4,128]{6,4,5,3,2,1,0:T(8,128)(2,1)S(1)}, u32[]{:S(2)}, u32[]{:S(2)}) collective-permute-start(bf16[1,1,4,16,16,4,128]{6,4,5,3,2,1,0:T(8,128)(2,1)S(1)} %bitcast.269), channel_id=1, source_target_pairs={{0,64},{64,128},{128,192},{1,65},{65,129},{129,193},{2,66},{66,130... | collective-permute-start | bytes 3145736 | tf_op jit(solution)/shard_map/ppermute | solution.py:15
  176.0 30.6 %copy-start.1 = (bf16[4,16,16,4,128]{4,2,3,1,0:T(8,128)(2,1)S(1)}, bf16[4,16,16,4,128]{4,2,3,1,0:T(8,128)(2,1)}, u32[]{:S(2)}) copy-start(bf16[4,16,16,4,128]{4,2,3,1,0:T(8,128)(2,1)} %fusion.124) | copy-start | bytes 3145732
  176.0 30.6 %copy-start.23 = (bf16[4,16,1,4,128]{4,2,3,1,0:T(2,128)(2,1)S(1)}, bf16[4,16,1,4,128]{4,2,3,1,0:T(2,128)(2,1)}, u32[]{:S(2)}) copy-start(bf16[4,16,1,4,128]{4,2,3,1,0:T(2,128)(2,1)} %copy-done.22) | copy-start | bytes 196612
  198.8 149.6 %collective-permute-start.7 = (bf16[3,1,4,16,16,4,128]{6,4,5,3,2,1,0:T(8,128)(2,1)}, bf16[3,1,4,16,16,4,128]{6,4,5,3,2,1,0:T(8,128)(2,1)}, u32[]{:S(2)}, u32[]{:S(2)}) collective-permute-start(bf16[3,1,4,16,16,4,128]{6,4,5,3,2,1,0:T(8,128)(2,1)} %pad_maximum_fusion.1), channel_id=1, source_target_pairs={{16,0},{32,16},{48,32},{17,1},{33,17},{49,33},{18,2},{34,18},{50,3... | collective-permute-start | bytes 9437192 | tf_op jit(solution)/shard_map/ppermute | solution.py:17
  200.1 148.3 %collective-permute-start.6 = (bf16[3,1,4,16,16,4,128]{6,4,5,3,2,1,0:T(8,128)(2,1)}, bf16[3,1,4,16,16,4,128]{6,4,5,3,2,1,0:T(8,128)(2,1)}, u32[]{:S(2)}, u32[]{:S(2)}) collective-permute-start(bf16[3,1,4,16,16,4,128]{6,4,5,3,2,1,0:T(8,128)(2,1)} %pad_maximum_fusion.1), channel_id=1, source_target_pairs={{0,16},{16,32},{32,48},{1,17},{17,33},{33,49},{2,18},{18,34},{34,5... | collective-permute-start | bytes 9437192 | tf_op jit(solution)/shard_map/ppermute | solution.py:15
  215.0 129.8 %all-to-all-start.1 = ((bf16[4,16,64,128]{3,1,0,2:T(8,128)(2,1)}), bf16[4,16,64,128]{3,1,0,2:T(8,128)(2,1)}, u32[]{:S(2)}, u32[]{:S(2)}) async-start(bf16[4,16,64,128]{3,1,0,2:T(8,128)(2,1)} %copy.160), calls=%async_computation.1 | async-start | bytes 2097152 | tf_op jit(solution)/shard_map/all_to_all | solution.py:171
  223.1 262.6 %all-reduce.6.cloned.1.call-start = ((), (), s32[]{:S(2)}) async-start(), calls=%async_computation.4 | async-start | bytes 1179648 | tf_op jit(solution)/shard_map/psum | solution.py:220
  364.7 18.4 %slice-start.1 = ((bf16[4,68,4,128]{3,2,1,0:T(4,128)(2,1)}), bf16[4,1,4,128]{3,2,1,0:T(4,128)(2,1)S(1)}, s32[]{:S(2)}) async-start(bf16[4,68,4,128]{3,2,1,0:T(4,128)(2,1)} %gather_fusion.15), calls=%async_computation.6 | async-start | bytes 8192 | tf_op jit(solution)/shard_map/slice | solution.py:55
  370.4 12.7 %slice-start = ((bf16[4,68,4,128]{3,2,1,0:T(4,128)(2,1)}), bf16[4,1,4,128]{3,2,1,0:T(4,128)(2,1)S(1)}, s32[]{:S(2)}) async-start(bf16[4,68,4,128]{3,2,1,0:T(4,128)(2,1)} %gather_fusion.13), calls=%async_computation.5 | async-start | bytes 8192 | tf_op jit(solution)/shard_map/slice | solution.py:55
  (18 other events, 35.7 us)
Sparse Core Ops, SparseCore 0:
  230.9 254.8 all-reduce.5
where the time goes:
time: 500 us; the launch traced here: 495 us
  waiting for transfers between devices  167 us (33%)
  blocking collectives  112 us (22%)
  local copies, waits for them, and re-layouts  80.4 us (16%)
  starting transfers between devices  63.5 us (13%)
  other arithmetic  33.4 us (7%)
  matrix products  22.8 us (5%)
  between operations  16.2 us (3%)
    psum x1, blocking collectives, body(): lax.psum((tap_part, depth_partial), ('gx', 'gy', 'gz'))  112 us
    psum x1, waiting for transfers between devices, body(): lax.psum((tap_part, depth_partial), ('gx', 'gy', 'gz'))  92.2 us
    gather x16, local copies, waits for them, and re-layouts, assemble(): chosen = [pooled[neighbor_ids[:, direction]] for direction in range(8)]  41.8 us
    ppermute x4, waiting for transfers between devices, padded_2(): lax.ppermute(head, axis, [((i + 1) % count, i) for i in range(ends)])  40.2 us
    ppermute x4, starting transfers between devices, padded_2(): lax.ppermute(tail, axis, [(i, (i + 1) % count) for i in range(ends)])  23.6 us
    all_to_all x2, waiting for transfers between devices, spread_slabs(): return lax.all_to_all(field, 'gz', split_axis=2, concat_axis=1, tiled=True)  22.8 us
    all_to_all x2, starting transfers between devices, gather_columns(): return lax.all_to_all(field, 'gz', split_axis=1, concat_axis=2, tiled=True)  21.7 us
    unnamed x92, local copies, waits for them, and re-layouts  16.5 us
  transfers between devices with their start and end apart: 13, of which 9 were waited for; matrix products, arithmetic and copies ran while one was open for 17% of the time, Pallas kernels for 0%

commit v1 on v0

v1 whole, which is shorter than its diff:
```python
import functools

import jax
import jax.numpy as jnp
from jax import lax
from jax.experimental import pallas as pl
from jax.experimental.pallas import tpu as pltpu
from jax.sharding import PartitionSpec as P

MESH = pl.DeviceIdType.MESH
F32 = jnp.float32
BF16 = jnp.bfloat16

SLOTS = 4
EDGE = 16
ZS = 4
LINE = EDGE * ZS
ROWS = EDGE * LINE
C = 128
GROUP = 4
PART = ROWS // GROUP
PLANE = 16
NZ = 16
CHIPS = 8
HALF = 5
TAPS = 9


def kernel(
    counts_hbm,
    nbr_hbm,
    act_hbm,
    cot_hbm,
    w_hbm,
    dw_hbm,
    out_hbm,
    ig_hbm,
    tg_hbm,
    dg_hbm,
    counts_ref,
    nbr_ref,
    act_v,
    cot_v,
    w_v,
    dw_ref,
    wbt,
    pad,
    xcat,
    gcat,
    gt,
    dsilu,
    active,
    cot_cols,
    back_send,
    back,
    act_cols,
    fwd_send,
    fwd,
    x_top,
    x_bot,
    x_left,
    x_right,
    g_top,
    g_bot,
    g_left,
    g_right,
    corner_send,
    corner_recv,
    col0,
    col1,
    corner_f,
    tacc,
    tp,
    rs_buf,
    z_src,
    c_buf,
    z_buf,
    z_all,
    dg_acc,
    dg_pair,
    dg_plane,
    dg_z,
    dg_out,
    load_sem,
    store_sem,
    halo_send,
    halo_recv,
    a2a_send,
    a2a_recv,
    pl_send,
    pl_recv,
    core_send,
    core_recv,
    chip_send,
    chip_recv,
):
    gx = lax.axis_index("gx")
    gy = lax.axis_index("gy")
    gz = lax.axis_index("gz")
    me_p = gx * 4 + gy
    q = gz // 4

    loads = [
        pltpu.make_async_copy(act_hbm, act_v, load_sem.at[0]),
        pltpu.make_async_copy(cot_hbm, cot_v, load_sem.at[1]),
        pltpu.make_async_copy(w_hbm, w_v, load_sem.at[2]),
        pltpu.make_async_copy(
            cot_hbm.at[:, pl.ds(pl.multiple_of(q * PART, PART), PART)], cot_cols.at[q], load_sem.at[3]
        ),
        pltpu.make_async_copy(dw_hbm, dw_ref, load_sem.at[4]),
        pltpu.make_async_copy(counts_hbm, counts_ref, load_sem.at[5]),
        pltpu.make_async_copy(nbr_hbm, nbr_ref, load_sem.at[6]),
    ]
    for load in loads:
        load.start()

    chip = gz // 2
    core = gz % 2

    def chip_peer(j):
        return {"gz": (gz + 2 * j) % NZ}

    core_peer = {"gz": gz + 1 - 2 * core}

    def p_peer(j):
        p = (me_p + j) % PLANE
        return {"gx": p // 4, "gy": p % 4}

    barrier = pltpu.get_barrier_semaphore()

    pl.semaphore_signal(barrier, inc=1, device_id=core_peer, device_id_type=MESH)
    for j in range(1, CHIPS):
        pl.semaphore_signal(barrier, inc=1, device_id=chip_peer(j), device_id_type=MESH)
    for j in range(1, PLANE):
        pl.semaphore_signal(barrier, inc=1, device_id=p_peer(j), device_id_type=MESH)
    pl.semaphore_wait(barrier, CHIPS + PLANE - 1)

    def group_peer(o):
        return {"gz": (gz + 4 * o) % NZ}

    def part_of(k):
        return pl.ds(pl.multiple_of(k * PART, PART), PART)

    def gather_copy(which, src, dst, s, o):
        k = (q + o) % GROUP
        return pltpu.make_async_remote_copy(
            src_ref=src.at[s, part_of(k)],
            dst_ref=dst.at[q, s],
            send_sem=a2a_send.at[which, s, o],
            recv_sem=a2a_recv.at[which, s, o],
            device_id=group_peer(o),
            device_id_type=MESH,
        )

    def spread_copy(which, src, dst, s, o):
        k = (q + o) % GROUP
        return pltpu.make_async_remote_copy(
            src_ref=src.at[k, s],
            dst_ref=dst.at[s, part_of(q)],
            send_sem=a2a_send.at[which, s, o],
            recv_sem=a2a_recv.at[which, s, o],
            device_id=group_peer(o),
            device_id_type=MESH,
        )

    cot_gather = functools.partial(gather_copy, 0, cot_hbm, cot_cols)
    back_spread = functools.partial(spread_copy, 1, back_send, back)
    act_gather = functools.partial(gather_copy, 2, active, act_cols)
    fwd_spread = functools.partial(spread_copy, 3, fwd_send, fwd)

    def start_all(copy, s):
        for o in range(1, GROUP):
            copy(s, o).start()

    def recv_all(copy, s):
        for o in range(1, GROUP):
            copy(s, o).wait_recv()

    for s in range(SLOTS):
        start_all(cot_gather, s)

    pools = ((x_top, x_bot, x_left, x_right), (g_top, g_bot, g_left, g_right))

    def halo_copies(f):
        def shift(axis, at, step):
            return {axis: (at + step + 4) % 4}

        def copy(k, src, dst, dev):
            return pltpu.make_async_remote_copy(
                src_ref=src,
                dst_ref=dst,
                send_sem=halo_send.at[f, k],
                recv_sem=halo_recv.at[f, k],
                device_id=dev,
                device_id_type=MESH,
            )

        result = []
        p_top, p_bot, p_left, p_right = pools[f]
        for k, (pool, axis, at, step) in enumerate(
            ((p_top, "gx", gx, 1), (p_bot, "gx", gx, -1), (p_left, "gy", gy, 1), (p_right, "gy", gy, -1))
        ):
            result.append(
                copy(k, pool.at[pl.ds(0, SLOTS)], pool.at[pl.ds(SLOTS, SLOTS)], shift(axis, at, step))
            )
        for k, (dx, dy) in enumerate(((1, 1), (1, -1), (-1, 1), (-1, -1))):
            dev = {**shift("gx", gx, dx), **shift("gy", gy, dy)}
            result.append(copy(4 + k, corner_send.at[f, k], corner_recv.at[f, k], dev))
        return result

    def own_pools(f):
        p_top, p_bot, p_left, p_right = pools[f]
        for s in range(SLOTS):
            p_bot[s] = pad[s, 1, 8 : 8 + LINE].astype(BF16)
            p_top[s] = pad[s, EDGE, 8 : 8 + LINE].astype(BF16)
            for x in range(EDGE):
                col0[ZS * x : ZS * x + ZS] = pad[s, 1 + x, 8:12]
                col1[ZS * x : ZS * x + ZS] = pad[s, 1 + x, 68:72]
            p_right[s] = col0[...].astype(BF16)
            p_left[s] = col1[...].astype(BF16)
            for k, (x, at) in enumerate(((EDGE, 68), (EDGE, 8), (1, 68), (1, 8))):
                corner_f[k, ZS * s : ZS * s + ZS] = pad[s, x, at : at + ZS]
        for k in range(4):
            corner_send[f, k] = corner_f[k].astype(BF16)
        for pool in (p_top, p_bot, p_left, p_right):
            pool[2 * SLOTS] = jnp.zeros((LINE, C), BF16)

    def entry(code, other):
        own = (code >= 16) & (code < 20)
        far = (code >= other) & (code < other + 4)
        return jnp.where(own, code - 16, jnp.where(far, code - other + 4, 8))

    def fill_halo(f, s):
        p_top, p_bot, p_left, p_right = pools[f]
        codes = [nbr_ref[s, d] for d in range(8)]
        pad[s, 0, 8 : 8 + LINE] = p_top[entry(codes[1], 4)].astype(F32)
        pad[s, EDGE + 1, 8 : 8 + LINE] = p_bot[entry(codes[6], 28)].astype(F32)
        col0[...] = p_left[entry(codes[3], 12)].astype(F32)
        col1[...] = p_right[entry(codes[4], 20)].astype(F32)
        for x in range(EDGE):
            pad[s, 1 + x, 4:8] = col0[ZS * x : ZS * x + ZS]
            pad[s, 1 + x, 72:76] = col1[ZS * x : ZS * x + ZS]
        for k, (d, row, at, pool_x, base_x, end_x, pool_y, base_y, end_y, base_c) in enumerate(
            (
                (0, 0, 4, p_top, 4, 1, p_left, 12, 1, 0),
                (2, 0, 72, p_top, 4, 0, p_right, 20, 1, 8),
                (5, EDGE + 1, 4, p_bot, 28, 1, p_left, 12, 0, 24),
                (7, EDGE + 1, 72, p_bot, 28, 0, p_right, 20, 0, 32),
            )
        ):
            code = codes[d]

            def piece(pool, base, end):
                low = (LINE - 16) * end
                rows = pool[entry(code, base), low : low + 16].astype(F32)
                return rows[12:16] if end else rows[0:4]

            via_x = piece(pool_x, base_x, end_x)
            via_y = piece(pool_y, base_y, end_y)
            tile = corner_recv[f, k].astype(F32)
            value = via_x
            value = jnp.where((code >= base_y) & (code < base_y + 4), via_y, value)
            for m in range(SLOTS):
                value = jnp.where(code == base_c + m, tile[ZS * m : ZS * m + ZS], value)
            pad[s, row, at : at + ZS] = value

    def lay_out(s, dst):
        for x in range(EDGE + 2):
            for j in range(3):
                at = 4 + ZS * j
                dst[s, x, :, C * j : C * j + C] = pad[s, x, at : at + LINE].astype(BF16)

    loads[0].wait()
    loads[5].wait()
    loads[6].wait()
    count = counts_ref[0, 0]

    def centre_x(s, carry):
        live = s < count
        for x in range(EDGE):
            rows = act_v[s, LINE * x : LINE * x + LINE].astype(F32)
            pad[s, 1 + x, 8 : 8 + LINE] = jnp.where(live, rows, 0.0)
        return carry

    lax.fori_loop(0, SLOTS, centre_x, 0)
    own_pools(0)
    x_halo = halo_copies(0)
    for copy in x_halo:
        copy.start()
    loads[2].wait()
    for i in range(3):
        for j in range(3):
            wbt[i, :, C * j : C * j + C] = w_v[3 * (2 - i) + 2 - j]

    for copy in x_halo:
        copy.wait_recv()

    def build_x(s, carry):
        fill_halo(0, s)
        lay_out(s, xcat)
        return carry

    lax.fori_loop(0, SLOTS, build_x, 0)

    def conv(n, carry):
        s = n // GROUP
        b = n % GROUP
        total = jnp.zeros((PART, C), F32)
        for i in range(3):
            window = xcat[s, pl.ds(4 * b + i, 4)].reshape(PART, 3 * C)
            weights = w_v[3 * i : 3 * i + 3].reshape(3 * C, C)
            total = total + jnp.dot(window, weights, preferred_element_type=F32)
        live = (s < count).astype(F32)
        sigma = jax.nn.sigmoid(total)
        active[s, part_of(b)] = (total * sigma * live).astype(BF16)
        dsilu[s, part_of(b)] = sigma * (1.0 + total * (1.0 - sigma)) * live
        return carry

    lax.fori_loop(0, SLOTS * GROUP, conv, 0)
    own_cols = pltpu.make_async_copy(active.at[:, part_of(q)], act_cols.at[q], load_sem.at[0])
    own_cols.start()

    loads[4].wait()
    taps = [dw_ref[t : t + 1].astype(F32) for t in range(5)]
    STEP = 32

    loads[3].wait()

    def depth_back(s):
        def step(n, carry):
            rows = pl.ds(pl.multiple_of(n * STEP, STEP), STEP)
            col = [cot_cols[k, s, rows].astype(F32) for k in range(GROUP)]
            for k in range(GROUP):
                total = None
                for t in range(5):
                    src = k - (t - 2)
                    if 0 <= src < GROUP:
                        term = taps[t] * col[src]
                        total = term if total is None else total + term
                back_send[k, s, rows] = total.astype(BF16)
            return carry

        lax.fori_loop(0, PART // STEP, step, 0)

    def do_back(s, carry):
        recv_all(cot_gather, s)
        depth_back(s)
        start_all(back_spread, s)
        back[s, part_of(q)] = back_send[q, s]
        return carry

    lax.fori_loop(0, SLOTS, do_back, 0)
    for s in range(SLOTS):
        start_all(act_gather, s)

    tacc[...] = jnp.zeros_like(tacc)

    def do_grad(s, carry):
        recv_all(back_spread, s)
        for x in range(EDGE):
            rows = pl.ds(LINE * x, LINE)
            grad = (back[s, rows].astype(F32) * dsilu[s, rows]).astype(BF16)
            gt[s, rows] = grad
            pad[s, 1 + x, 8 : 8 + LINE] = grad.astype(F32)
        return carry

    def tap_step(s, carry):
        grad_t = gt[s].T
        for i in range(3):
            window = xcat[s, i : i + EDGE].reshape(ROWS, 3 * C)
            tacc[i] += jnp.dot(grad_t, window, preferred_element_type=F32)
        return carry

    def grad_slot(s, carry):
        do_grad(s, 0)
        tap_step(s, 0)
        return carry

    lax.fori_loop(0, SLOTS - 1, grad_slot, 0)
    do_grad(SLOTS - 1, 0)
    own_pools(1)
    g_halo = halo_copies(1)
    for copy in g_halo:
        copy.start()
    tap_step(SLOTS - 1, 0)
    for i in range(3):
        for j in range(3):
            block = tacc[i, :, C * j : C * j + C].T
            tp[:, 3 * i + j] = block.reshape(PLANE, 8, C)

    def plane_scatter(j):
        p = (me_p + j) % PLANE
        return pltpu.make_async_remote_copy(
            src_ref=tp.at[p],
            dst_ref=rs_buf.at[me_p],
            send_sem=pl_send.at[0, j],
            recv_sem=pl_recv.at[0, j],
            device_id=p_peer(j),
            device_id_type=MESH,
        )

    def plane_gather(j):
        return pltpu.make_async_remote_copy(
            src_ref=z_all.at[pl.ds(0, TAPS)],
            dst_ref=tg_hbm.at[:, me_p],
            send_sem=pl_send.at[1, j],
            recv_sem=pl_recv.at[1, j],
            device_id=p_peer(j),
            device_id_type=MESH,
        )

    def plane_depth(j):
        return pltpu.make_async_remote_copy(
            src_ref=dg_plane.at[me_p],
            dst_ref=dg_plane.at[me_p],
            send_sem=pl_send.at[2, j],
            recv_sem=pl_recv.at[2, j],
            device_id=p_peer(j),
            device_id_type=MESH,
        )

    def core_copy(n, src, dst):
        return pltpu.make_async_remote_copy(
            src_ref=src,
            dst_ref=dst,
            send_sem=core_send.at[n],
            recv_sem=core_recv.at[n],
            device_id=core_peer,
            device_id_type=MESH,
        )

    core_scatter = core_copy(0, z_src.at[pl.ds(HALF * (1 - core), HALF)], c_buf)
    core_gather = core_copy(1, z_all.at[pl.ds(HALF * core, HALF)], z_all.at[pl.ds(HALF * core, HALF)])
    core_depth = core_copy(2, dg_pair.at[core], dg_pair.at[core])

    def chip_copy(n, src, dst, j):
        return pltpu.make_async_remote_copy(
            src_ref=src,
            dst_ref=dst,
            send_sem=chip_send.at[n, j],
            recv_sem=chip_recv.at[n, j],
            device_id=chip_peer(j),
            device_id_type=MESH,
        )

    def chip_gather(j):
        return chip_copy(0, z_buf.at[chip], z_buf.at[chip], j)

    def chip_depth(j):
        return chip_copy(1, dg_z.at[chip], dg_z.at[chip], j)

    def each(copy, action, stop=PLANE):
        def step(j, carry):
            getattr(copy(j), action)()
            return carry

        lax.fori_loop(1, stop, step, 0)

    each(plane_scatter, "start")

    own_cols.wait()
    dg_acc[...] = jnp.zeros_like(dg_acc)

    def depth_forward(s):
        def step(n, carry):
            rows = pl.ds(pl.multiple_of(n * STEP, STEP), STEP)
            col = [act_cols[k, s, rows].astype(F32) for k in range(GROUP)]
            cot = [cot_cols[k, s, rows].astype(F32) for k in range(GROUP)]
            sums = [None] * 5
            for k in range(GROUP):
                total = None
                for t in range(5):
                    src = k + t - 2
                    if 0 <= src < GROUP:
                        term = taps[t] * col[src]
                        total = term if total is None else total + term
                        grad = col[src] * cot[k]
                        sums[t] = grad if sums[t] is None else sums[t] + grad
                fwd_send[k, s, rows] = total.astype(BF16)
            for t in range(5):
                dg_acc[t] += jnp.sum(sums[t].reshape(STEP // 8, 8, C), axis=0)
            return carry

        lax.fori_loop(0, PART // STEP, step, 0)

    def do_forward(s):
        recv_all(act_gather, s)
        depth_forward(s)
        start_all(fwd_spread, s)
        fwd[s, part_of(q)] = fwd_send[q, s]

    do_forward(0)

    for copy in g_halo:
        copy.wait_recv()

    def build_g(s, carry):
        fill_halo(1, s)
        lay_out(s, gcat)
        return carry

    lax.fori_loop(0, SLOTS, build_g, 0)

    loads[1].wait()

    def conv_back(n, carry):
        s = n // GROUP
        b = n % GROUP
        total = jnp.zeros((PART, C), F32)
        for i in range(3):
            window = gcat[s, pl.ds(4 * b + i, 4)].reshape(PART, 3 * C)
            total = total + lax.dot_general(
                window, wbt[i], (((1,), (1,)), ((), ())), preferred_element_type=F32
            )
        live = (s < count).astype(F32)
        rows = part_of(b)
        cot_v[s, rows] = ((cot_v[s, rows].astype(F32) + total) * live).astype(BF16)
        return carry

    lax.fori_loop(0, 2 * GROUP, conv_back, 0)

    rs_buf[me_p] = tp[me_p]
    z_src[...] = jnp.zeros_like(z_src)
    each(plane_scatter, "wait_recv")
    part_sum = rs_buf[0]
    for p in range(1, PLANE):
        part_sum = part_sum + rs_buf[p]
    z_src[0:TAPS] = part_sum
    core_scatter.start()
    core_scatter.wait_recv()
    z_buf[chip] = z_src[pl.ds(HALF * core, HALF)] + c_buf[...]
    each(chip_gather, "start", CHIPS)

    do_forward(1)
    lax.fori_loop(2 * GROUP, SLOTS * GROUP, conv_back, 0)
    ig_store = pltpu.make_async_copy(cot_v, ig_hbm, store_sem.at[0])
    ig_store.start()
    do_forward(2)
    do_forward(3)
    dg_pair[core] = jnp.concatenate(
        [jnp.sum(dg_acc[t], axis=0, keepdims=True) for t in range(5)] + [jnp.zeros((3, C), F32)], axis=0
    )
    core_depth.start()
    core_depth.wait_recv()
    dg_plane[me_p] = dg_pair[0] + dg_pair[1]
    each(plane_depth, "start")
    each(plane_depth, "wait_recv")
    dg_sum = dg_plane[0]
    for p in range(1, PLANE):
        dg_sum = dg_sum + dg_plane[p]
    dg_z[chip] = dg_sum
    each(chip_depth, "start", CHIPS)

    each(chip_gather, "wait_recv", CHIPS)
    z_sum = z_buf[0]
    for k in range(1, CHIPS):
        z_sum = z_sum + z_buf[k]
    z_all[pl.ds(HALF * core, HALF)] = z_sum
    core_gather.start()
    core_gather.wait_recv()
    each(plane_gather, "start")
    tg_own = pltpu.make_async_copy(z_all.at[pl.ds(0, TAPS)], tg_hbm.at[:, me_p], store_sem.at[1])
    tg_own.start()

    def out_store(s):
        return pltpu.make_async_copy(act_v.at[s], out_hbm.at[s], store_sem.at[2 + s])

    def finish(s, carry):
        recv_all(fwd_spread, s)
        live = s < count
        for b in range(GROUP):
            rows = pl.ds(PART * b, PART)
            masked = jnp.where(live, act_v[s, rows].astype(F32), 0.0)
            act_v[s, rows] = (masked + fwd[s, rows].astype(F32)).astype(BF16)
        out_store(s).start()
        return carry

    lax.fori_loop(0, SLOTS - 1, finish, 0)
    each(chip_depth, "wait_recv", CHIPS)
    dg_all = dg_z[0]
    for k in range(1, CHIPS):
        dg_all = dg_all + dg_z[k]
    dg_out[...] = dg_all[0:5]
    dg_store = pltpu.make_async_copy(dg_out, dg_hbm, store_sem.at[6])
    dg_store.start()
    finish(SLOTS - 1, 0)
    each(plane_gather, "wait_recv")

    for copy in x_halo + g_halo:
        copy.wait_send()
    for copy in (cot_gather, back_spread, act_gather, fwd_spread):
        for s in range(SLOTS):
            for o in range(1, GROUP):
                copy(s, o).wait_send()
    for copy in (plane_scatter, plane_gather, plane_depth):
        each(copy, "wait_send")
    for copy in (chip_gather, chip_depth):
        each(copy, "wait_send", CHIPS)
    for copy in (core_scatter, core_gather, core_depth):
        copy.wait_send()
    ig_store.wait()
    tg_own.wait()
    dg_store.wait()
    for s in range(SLOTS):
        out_store(s).wait()


def copy_out(*refs):
    src, dst, buf, load_sem, store_sem = refs[0:4], refs[4:8], refs[8:12], refs[12], refs[13]
    steps = [(0, s) for s in range(SLOTS)] + [(1, s) for s in range(SLOTS)] + [(2, s) for s in range(3)] + [(3, 0)]

    def at(k, ref, s):
        return ref.at[s] if k < 2 else ref.at[pl.ds(3 * s, 3)] if k == 2 else ref

    loads, stores = [], []
    for n, (k, s) in enumerate(steps):
        loads.append(pltpu.make_async_copy(at(k, src[k], s), at(k, buf[k], s), load_sem.at[n]))
        stores.append(pltpu.make_async_copy(at(k, buf[k], s), at(k, dst[k], s), store_sem.at[n]))
    for load in loads:
        load.start()
    for load, store in zip(loads, stores):
        load.wait()
        store.start()
    for store in stores:
        store.wait()


def body(activations, cotangent, tap_weights, depth_tap_weight, counts, neighbors):
    field = (SLOTS, ROWS, C)
    anywhere = pl.BlockSpec(memory_space=pl.ANY)
    results = pl.pallas_call(
        kernel,
        out_shape=[
            jax.ShapeDtypeStruct(field, BF16),
            jax.ShapeDtypeStruct(field, BF16),
            jax.ShapeDtypeStruct((TAPS, PLANE, 8, C), F32),
            jax.ShapeDtypeStruct((5, C), F32),
        ],
        in_specs=[anywhere] * 6,
        out_specs=[anywhere] * 4,
        scratch_shapes=[
            pltpu.SMEM((1, 1), jnp.int32),
            pltpu.SMEM((SLOTS, 8), jnp.int32),
            pltpu.VMEM(field, BF16),
            pltpu.VMEM(field, BF16),
            pltpu.VMEM((TAPS, C, C), BF16),
            pltpu.VMEM((5, C), BF16),
            pltpu.VMEM((3, C, 3 * C), BF16),
            pltpu.VMEM((SLOTS, EDGE + 2, LINE + 16, C), F32),
            pltpu.VMEM((SLOTS, EDGE + 2, LINE, 3 * C), BF16),
            pltpu.VMEM((SLOTS, EDGE + 2, LINE, 3 * C), BF16),
            pltpu.VMEM(field, BF16),
            pltpu.VMEM(field, F32),
            pltpu.VMEM(field, BF16),
            pltpu.VMEM((GROUP, SLOTS, PART, C), BF16),
            pltpu.VMEM((GROUP, SLOTS, PART, C), BF16),
            pltpu.VMEM(field, BF16),
            pltpu.VMEM((GROUP, SLOTS, PART, C), BF16),
            pltpu.VMEM((GROUP, SLOTS, PART, C), BF16),
            pltpu.VMEM(field, BF16),
            pltpu.VMEM((2 * SLOTS + 1, LINE, C), BF16),
            pltpu.VMEM((2 * SLOTS + 1, LINE, C), BF16),
            pltpu.VMEM((2 * SLOTS + 1, LINE, C), BF16),
            pltpu.VMEM((2 * SLOTS + 1, LINE, C), BF16),
            pltpu.VMEM((2 * SLOTS + 1, LINE, C), BF16),
            pltpu.VMEM((2 * SLOTS + 1, LINE, C), BF16),
            pltpu.VMEM((2 * SLOTS + 1, LINE, C), BF16),
            pltpu.VMEM((2 * SLOTS + 1, LINE, C), BF16),
            pltpu.VMEM((2, 4, 16, C), BF16),
            pltpu.VMEM((2, 4, 16, C), BF16),
            pltpu.VMEM((LINE, C), F32),
            pltpu.VMEM((LINE, C), F32),
            pltpu.VMEM((4, 16, C), F32),
            pltpu.VMEM((3, C, 3 * C), F32),
            pltpu.VMEM((PLANE, TAPS, 8, C), F32),
            pltpu.VMEM((PLANE, TAPS, 8, C), F32),
            pltpu.VMEM((2 * HALF, 8, C), F32),
            pltpu.VMEM((HALF, 8, C), F32),
            pltpu.VMEM((CHIPS, HALF, 8, C), F32),
            pltpu.VMEM((2 * HALF, 8, C), F32),
            pltpu.VMEM((5, 8, C), F32),
            pltpu.VMEM((2, 8, C), F32),
            pltpu.VMEM((PLANE, 8, C), F32),
            pltpu.VMEM((CHIPS, 8, C), F32),
            pltpu.VMEM((5, C), F32),
            pltpu.SemaphoreType.DMA((7,)),
            pltpu.SemaphoreType.DMA((7,)),
            pltpu.SemaphoreType.DMA((2, 8)),
            pltpu.SemaphoreType.DMA((2, 8)),
            pltpu.SemaphoreType.DMA((4, SLOTS, GROUP)),
            pltpu.SemaphoreType.DMA((4, SLOTS, GROUP)),
            pltpu.SemaphoreType.DMA((3, PLANE)),
            pltpu.SemaphoreType.DMA((3, PLANE)),
            pltpu.SemaphoreType.DMA((3,)),
            pltpu.SemaphoreType.DMA((3,)),
            pltpu.SemaphoreType.DMA((2, CHIPS)),
            pltpu.SemaphoreType.DMA((2, CHIPS)),
        ],
        compiler_params=pltpu.CompilerParams(
            collective_id=0, has_side_effects=True, vmem_limit_bytes=60 * 2**20
        ),
        name="unet_section",
    )(
        counts,
        neighbors.reshape(SLOTS, 8),
        activations.reshape(field),
        cotangent.reshape(field),
        tap_weights,
        depth_tap_weight,
    )
    output, input_grad, tap_grad, depth_grad = pl.pallas_call(
        copy_out,
        out_shape=[jax.ShapeDtypeStruct(r.shape, r.dtype) for r in results],
        in_specs=[anywhere] * 4,
        out_specs=[anywhere] * 4,
        scratch_shapes=[pltpu.VMEM(r.shape, r.dtype) for r in results]
        + [pltpu.SemaphoreType.DMA((12,)), pltpu.SemaphoreType.DMA((12,))],
        compiler_params=pltpu.CompilerParams(vmem_limit_bytes=60 * 2**20),
        name="copy_out",
    )(*results)
    return (
        output.reshape(activations.shape),
        input_grad.reshape(activations.shape),
        tap_grad.reshape(TAPS, C, C),
        depth_grad,
    )


def solution(mesh):
    field = P("gx", "gy", None, None, None, "gz", None)
    return jax.shard_map(
        body,
        mesh=mesh,
        in_specs=(field, field, P(), P(), P("gx", "gy"), P("gx", "gy", None, None)),
        out_specs=(field, field, P(), P()),
        check_vma=False,
    )
```

time: 500 us -> 122 us (0.24)
  waiting for transfers between devices: 167 us -> 0 us
  Pallas kernels: 0 us -> 120 us
  blocking collectives: 112 us -> 0 us
  local copies, waits for them, and re-layouts: 80.4 us -> 0 us
  starting transfers between devices: 63.5 us -> 0 us
  other arithmetic: 33.4 us -> 0 us
  matrix products: 22.8 us -> 0 us
  between operations: 16.2 us -> 1.29 us
    pallas_call x0 -> x2, Pallas kernels: none -> 120 us  [the longest x1 118 us: body(): pl.pallas_call(kernel, out_shape=[jax.ShapeDtypeStruct(field, BF16), jax....]
    psum x1 -> x0, blocking collectives: 112 us -> none  [body(): lax.psum((tap_part, depth_partial), ('gx', 'gy', 'gz'))]
    psum x1 -> x0, waiting for transfers between devices: 92.2 us -> none  [body(): lax.psum((tap_part, depth_partial), ('gx', 'gy', 'gz'))]
    ppermute x8 -> x0, waiting for transfers between devices: 42.9 us -> none  [the longest x4 40.2 us: padded_2(): lax.ppermute(head, axis, [((i + 1) % count, i) for i in range(ends)])]
    gather x16 -> x0, local copies, waits for them, and re-layouts: 41.8 us -> none  [assemble(): chosen = [pooled[neighbor_ids[:, direction]] for direction in range(8)]]
    all_to_all x4 -> x0, starting transfers between devices: 34.7 us -> none  [the longest x2 21.7 us: gather_columns(): return lax.all_to_all(field, 'gz', split_axis=1, concat_axis=2, tiled=True)]
    all_to_all x4 -> x0, waiting for transfers between devices: 31.8 us -> none  [the longest x2 22.8 us: spread_slabs(): return lax.all_to_all(field, 'gz', split_axis=2, concat_axis=1, tiled=True)]
    ppermute x8 -> x0, starting transfers between devices: 28.8 us -> none  [the longest x4 23.6 us: padded_2(): lax.ppermute(tail, axis, [(i, (i + 1) % count) for i in range(ends)])]
  transfers between devices with their start and end apart: 13 -> 0, of which waited for: 9 -> 0; matrix products, arithmetic and copies ran while one was open for 17% -> 0% of each run, Pallas kernels for 0% -> 0%
where the time goes in v1:
time: 122 us
  Pallas kernels  120 us (98%)
  between operations  1.29 us (1%)
    pallas_call x1, Pallas kernels, body(): pl.pallas_call(kernel, out_shape=[jax.ShapeDtypeStruct(field, BF16), jax....  118 us
    pallas_call x1, Pallas kernels, body(): pl.pallas_call(copy_out, out_shape=[jax.ShapeDtypeStruct(r.shape, r.dtype...  2.66 us

profile of v1, /device:TPU:1, one launch (start us, length us, event | category | flops | bytes accessed | tf_op | source)
XLA Modules:
  0.0 121.5 jit_solution(1063281820277984545)
XLA Ops:
  1.3 117.6 %unet_section.1 = (bf16[4,1024,128]{2,1,0:T(8,128)(2,1)}, bf16[4,1024,128]{2,1,0:T(8,128)(2,1)}, f32[9,16,8,128]{3,2,1,0:T(8,128)}, f32[5,128]{1,0:T(8,128)}) custom-call(s32[1,1]{1,0:T(1,128)S(6)} %copy.10.counts_hbm, s32[4,8]{1,0:T(4,128)} %bitcast.8, bf16[4,1024,128]{2,1,0:T(8,128)(2,1)} %bitcast.6, bf16[4,1024,128]{2,1,0:T(8,128)(2,1)} %bitcast.7, ...), custom_call_target="tpu_custom_call" | custom-call | tf_op jit(solution)/shard_map/unet_section/pallas_call | solution.py:631
  118.9 2.7 %copy_out.1 = (bf16[4,1024,128]{2,1,0:T(8,128)(2,1)}, bf16[4,1024,128]{2,1,0:T(8,128)(2,1)}, f32[9,16,8,128]{3,2,1,0:T(8,128)}, f32[5,128]{1,0:T(8,128)}) custom-call(bf16[4,1024,128]{2,1,0:T(8,128)(2,1)} %get-tuple-element.12.refs_0_, bf16[4,1024,128]{2,1,0:T(8,128)(2,1)} %get-tuple-element.13.refs_1_, f32[9,16,8,128]{3,2,1,0:T(8,128)} %get-tuple-element.14.refs_2_, ...), custom_call_target="tpu_custom_call" | custom-call | tf_op jit(solution)/shard_map/copy_out/pallas_call | solution.py:711

commit v2 on v1

--- a/solution.py
+++ b/solution.py
@@ -24,6 +24,8 @@
 CHIPS = 8
 HALF = 5
 TAPS = 9
+PIECE = 80
+ZPIECE = 48
 
 
 def kernel(
@@ -71,11 +73,13 @@
     corner_f,
     tacc,
     tp,
+    tp_send,
     rs_buf,
     z_src,
     c_buf,
     z_buf,
     z_all,
+    tg_send,
     dg_acc,
     dg_pair,
     dg_plane,
@@ -350,8 +354,6 @@
         return carry
 
     lax.fori_loop(0, SLOTS, do_back, 0)
-    for s in range(SLOTS):
-        start_all(act_gather, s)
 
     tacc[...] = jnp.zeros_like(tacc)
 
@@ -373,6 +375,7 @@
 
     def grad_slot(s, carry):
         do_grad(s, 0)
+        start_all(act_gather, s)
         tap_step(s, 0)
         return carry
 
@@ -382,16 +385,20 @@
     g_halo = halo_copies(1)
     for copy in g_halo:
         copy.start()
+    start_all(act_gather, SLOTS - 1)
     tap_step(SLOTS - 1, 0)
     for i in range(3):
         for j in range(3):
             block = tacc[i, :, C * j : C * j + C].T
             tp[:, 3 * i + j] = block.reshape(PLANE, 8, C)
+    tp[:, TAPS] = jnp.zeros((PLANE, 8, C), F32)
+    for p in range(PLANE):
+        tp_send[p] = tp[p].reshape(PIECE, C).astype(BF16)
 
     def plane_scatter(j):
         p = (me_p + j) % PLANE
         return pltpu.make_async_remote_copy(
-            src_ref=tp.at[p],
+            src_ref=tp_send.at[p],
             dst_ref=rs_buf.at[me_p],
             send_sem=pl_send.at[0, j],
             recv_sem=pl_recv.at[0, j],
@@ -401,8 +408,8 @@
 
     def plane_gather(j):
         return pltpu.make_async_remote_copy(
-            src_ref=z_all.at[pl.ds(0, TAPS)],
-            dst_ref=tg_hbm.at[:, me_p],
+            src_ref=tg_send,
+            dst_ref=tg_hbm.at[me_p],
             send_sem=pl_send.at[1, j],
             recv_sem=pl_recv.at[1, j],
             device_id=p_peer(j),
@@ -489,8 +496,6 @@
         start_all(fwd_spread, s)
         fwd[s, part_of(q)] = fwd_send[q, s]
 
-    do_forward(0)
-
     for copy in g_halo:
         copy.wait_recv()
 
@@ -517,24 +522,36 @@
         cot_v[s, rows] = ((cot_v[s, rows].astype(F32) + total) * live).astype(BF16)
         return carry
 
-    lax.fori_loop(0, 2 * GROUP, conv_back, 0)
-
-    rs_buf[me_p] = tp[me_p]
-    z_src[...] = jnp.zeros_like(z_src)
+
+    rs_buf[me_p] = tp_send[me_p]
     each(plane_scatter, "wait_recv")
-    part_sum = rs_buf[0]
+    part_sum = rs_buf[0].astype(F32)
     for p in range(1, PLANE):
-        part_sum = part_sum + rs_buf[p]
-    z_src[0:TAPS] = part_sum
+        part_sum = part_sum + rs_buf[p].astype(F32)
+    z_src[...] = part_sum.reshape(2 * HALF, 8, C)
     core_scatter.start()
     core_scatter.wait_recv()
-    z_buf[chip] = z_src[pl.ds(HALF * core, HALF)] + c_buf[...]
+    z_own = (z_src[pl.ds(HALF * core, HALF)] + c_buf[...]).reshape(8 * HALF, C)
+    z_buf[chip] = jnp.concatenate([z_own, jnp.zeros((ZPIECE - 8 * HALF, C), F32)], axis=0).astype(BF16)
     each(chip_gather, "start", CHIPS)
-
+    do_forward(0)
     do_forward(1)
-    lax.fori_loop(2 * GROUP, SLOTS * GROUP, conv_back, 0)
+    lax.fori_loop(0, SLOTS * GROUP, conv_back, 0)
     ig_store = pltpu.make_async_copy(cot_v, ig_hbm, store_sem.at[0])
     ig_store.start()
+
+    each(chip_gather, "wait_recv", CHIPS)
+    z_sum = z_buf[0].astype(F32)
+    for k in range(1, CHIPS):
+        z_sum = z_sum + z_buf[k].astype(F32)
+    z_all[pl.ds(HALF * core, HALF)] = z_sum[0 : 8 * HALF].reshape(HALF, 8, C)
+    core_gather.start()
+    core_gather.wait_recv()
+    tg_send[...] = z_all[...].reshape(PIECE, C).astype(BF16)
+    each(plane_gather, "start")
+    tg_own = pltpu.make_async_copy(tg_send, tg_hbm.at[me_p], store_sem.at[1])
+    tg_own.start()
+
     do_forward(2)
     do_forward(3)
     dg_pair[core] = jnp.concatenate(
@@ -551,17 +568,6 @@
     dg_z[chip] = dg_sum
     each(chip_depth, "start", CHIPS)
 
-    each(chip_gather, "wait_recv", CHIPS)
-    z_sum = z_buf[0]
-    for k in range(1, CHIPS):
-        z_sum = z_sum + z_buf[k]
-    z_all[pl.ds(HALF * core, HALF)] = z_sum
-    core_gather.start()
-    core_gather.wait_recv()
-    each(plane_gather, "start")
-    tg_own = pltpu.make_async_copy(z_all.at[pl.ds(0, TAPS)], tg_hbm.at[:, me_p], store_sem.at[1])
-    tg_own.start()
-
     def out_store(s):
         return pltpu.make_async_copy(act_v.at[s], out_hbm.at[s], store_sem.at[2 + s])
 
@@ -575,7 +581,7 @@
         out_store(s).start()
         return carry
 
-    lax.fori_loop(0, SLOTS - 1, finish, 0)
+    lax.fori_loop(0, SLOTS, finish, 0)
     each(chip_depth, "wait_recv", CHIPS)
     dg_all = dg_z[0]
     for k in range(1, CHIPS):
@@ -583,7 +589,6 @@
     dg_out[...] = dg_all[0:5]
     dg_store = pltpu.make_async_copy(dg_out, dg_hbm, store_sem.at[6])
     dg_store.start()
-    finish(SLOTS - 1, 0)
     each(plane_gather, "wait_recv")
 
     for copy in x_halo + g_halo:
@@ -606,19 +611,24 @@
 
 
 def copy_out(*refs):
-    src, dst, buf, load_sem, store_sem = refs[0:4], refs[4:8], refs[8:12], refs[12], refs[13]
-    steps = [(0, s) for s in range(SLOTS)] + [(1, s) for s in range(SLOTS)] + [(2, s) for s in range(3)] + [(3, 0)]
-
-    def at(k, ref, s):
-        return ref.at[s] if k < 2 else ref.at[pl.ds(3 * s, 3)] if k == 2 else ref
-
-    loads, stores = [], []
-    for n, (k, s) in enumerate(steps):
-        loads.append(pltpu.make_async_copy(at(k, src[k], s), at(k, buf[k], s), load_sem.at[n]))
-        stores.append(pltpu.make_async_copy(at(k, buf[k], s), at(k, dst[k], s), store_sem.at[n]))
+    src, dst, buf, tap_buf, load_sem, store_sem = refs[0:4], refs[4:8], refs[8:12], refs[12], refs[13], refs[14]
+    loads = [pltpu.make_async_copy(src[2], buf[2], load_sem.at[0]), pltpu.make_async_copy(src[3], buf[3], load_sem.at[1])]
+    stores = []
+    for k in range(2):
+        for s in range(SLOTS):
+            n = 2 + SLOTS * k + s
+            loads.append(pltpu.make_async_copy(src[k].at[s], buf[k].at[s], load_sem.at[n]))
+            stores.append(pltpu.make_async_copy(buf[k].at[s], dst[k].at[s], store_sem.at[n]))
+    stores += [pltpu.make_async_copy(tap_buf, dst[2], store_sem.at[0]), pltpu.make_async_copy(buf[3], dst[3], store_sem.at[1])]
     for load in loads:
         load.start()
-    for load, store in zip(loads, stores):
+    loads[0].wait()
+    for p in range(PLANE):
+        tap_buf[:, p] = buf[2][p].astype(F32)[0 : 8 * TAPS].reshape(TAPS, 8, C)
+    stores[-2].start()
+    loads[1].wait()
+    stores[-1].start()
+    for load, store in zip(loads[2:], stores[:-2]):
         load.wait()
         store.start()
     for store in stores:
@@ -633,7 +643,7 @@
         out_shape=[
             jax.ShapeDtypeStruct(field, BF16),
             jax.ShapeDtypeStruct(field, BF16),
-            jax.ShapeDtypeStruct((TAPS, PLANE, 8, C), F32),
+            jax.ShapeDtypeStruct((PLANE, PIECE, C), BF16),
             jax.ShapeDtypeStruct((5, C), F32),
         ],
         in_specs=[anywhere] * 6,
@@ -672,12 +682,14 @@
             pltpu.VMEM((LINE, C), F32),
             pltpu.VMEM((4, 16, C), F32),
             pltpu.VMEM((3, C, 3 * C), F32),
-            pltpu.VMEM((PLANE, TAPS, 8, C), F32),
-            pltpu.VMEM((PLANE, TAPS, 8, C), F32),
+            pltpu.VMEM((PLANE, 2 * HALF, 8, C), F32),
+            pltpu.VMEM((PLANE, PIECE, C), BF16),
+            pltpu.VMEM((PLANE, PIECE, C), BF16),
             pltpu.VMEM((2 * HALF, 8, C), F32),
             pltpu.VMEM((HALF, 8, C), F32),
-            pltpu.VMEM((CHIPS, HALF, 8, C), F32),
+            pltpu.VMEM((CHIPS, ZPIECE, C), BF16),
             pltpu.VMEM((2 * HALF, 8, C), F32),
+            pltpu.VMEM((PIECE, C), BF16),
             pltpu.VMEM((5, 8, C), F32),
             pltpu.VMEM((2, 8, C), F32),
             pltpu.VMEM((PLANE, 8, C), F32),
@@ -710,11 +722,20 @@
     )
     output, input_grad, tap_grad, depth_grad = pl.pallas_call(
         copy_out,
-        out_shape=[jax.ShapeDtypeStruct(r.shape, r.dtype) for r in results],
+        out_shape=[
+            jax.ShapeDtypeStruct(field, BF16),
+            jax.ShapeDtypeStruct(field, BF16),
+            jax.ShapeDtypeStruct((TAPS, PLANE, 8, C), F32),
+            jax.ShapeDtypeStruct((5, C), F32),
+        ],
         in_specs=[anywhere] * 4,
         out_specs=[anywhere] * 4,
         scratch_shapes=[pltpu.VMEM(r.shape, r.dtype) for r in results]
-        + [pltpu.SemaphoreType.DMA((12,)), pltpu.SemaphoreType.DMA((12,))],
+        + [
+            pltpu.VMEM((TAPS, PLANE, 8, C), F32),
+            pltpu.SemaphoreType.DMA((10,)),
+            pltpu.SemaphoreType.DMA((10,)),
+        ],
         compiler_params=pltpu.CompilerParams(vmem_limit_bytes=60 * 2**20),
         name="copy_out",
     )(*results)

time: 122 us -> 117 us (0.959)
  Pallas kernels: 120 us -> 115 us
    pallas_call x1, Pallas kernels: 118 us -> 112 us  [body(): pl.pallas_call(kernel, out_shape=[jax.ShapeDtypeStruct(field, BF16), jax....]
where the time goes in v2:
time: 117 us; the launch traced here: 116 us
  Pallas kernels  115 us (98%)
  between operations  1.29 us (1%)
    pallas_call x1, Pallas kernels, body(): pl.pallas_call(kernel, out_shape=[jax.ShapeDtypeStruct(field, BF16), jax....  112 us
    pallas_call x1, Pallas kernels, body(): pl.pallas_call(copy_out, out_shape=[jax.ShapeDtypeStruct(field, BF16), ja...  2.7 us

profile of v2, /device:TPU:1, one launch (start us, length us, event | category | flops | bytes accessed | tf_op | source)
XLA Modules:
  0.0 116.0 jit_solution(2225655146030859495)
XLA Ops:
  1.3 112.0 %unet_section.1 = (bf16[4,1024,128]{2,1,0:T(8,128)(2,1)}, bf16[4,1024,128]{2,1,0:T(8,128)(2,1)}, bf16[16,80,128]{2,1,0:T(8,128)(2,1)}, f32[5,128]{1,0:T(8,128)}) custom-call(s32[1,1]{1,0:T(1,128)S(6)} %copy.10.counts_hbm, s32[4,8]{1,0:T(4,128)} %bitcast.8, bf16[4,1024,128]{2,1,0:T(8,128)(2,1)} %bitcast.6, bf16[4,1024,128]{2,1,0:T(8,128)(2,1)} %bitcast.7, ...), custom_call_target="tpu_custom_call" | custom-call | tf_op jit(solution)/shard_map/unet_section/pallas_call | solution.py:641
  113.3 2.7 %copy_out.1 = (bf16[4,1024,128]{2,1,0:T(8,128)(2,1)}, bf16[4,1024,128]{2,1,0:T(8,128)(2,1)}, f32[9,16,8,128]{3,2,1,0:T(8,128)}, f32[5,128]{1,0:T(8,128)}) custom-call(bf16[4,1024,128]{2,1,0:T(8,128)(2,1)} %get-tuple-element.12.refs_0_, bf16[4,1024,128]{2,1,0:T(8,128)(2,1)} %get-tuple-element.13.refs_1_, bf16[16,80,128]{2,1,0:T(8,128)(2,1)} %get-tuple-element.14.refs_2_, ...), custom_call_target="tpu_custom_call" | custom-call | tf_op jit(solution)/shard_map/copy_out/pallas_call | solution.py:723
